TPU v7x, 32 devices: a whole 2x2x4 slice. The times are simulated.
32 devices in a mesh: row: 16 (over z, y, core), col: 2 (over x).
Axes of the slice: x: 2, y: 2, z: 4, core: 2. Of those that a mesh axis runs over, the one named last changes fastest.
Arguments:
- features: bfloat16 [128, 4096], P(None, ('row', 'col')), may hold values from -6 to 6
- positions: float32 [3, 4096], P(None, ('row', 'col')), may hold values from 0 to 6
- tile_pairs: int32 [16, 2, 2, 4], P('row', 'col'), may hold values from 0 to 15, as said below
- pair_count: int32 [16, 2], P('row', 'col'), may hold values from 1 to 4, as said below
- masks: int32 [16, 2, 4, 128, 128], P('row', 'col'), may hold values 0 or 1
- w_in: bfloat16 [128, 128], replicated, may hold values from -0.5 to 0.5
- w_f1: bfloat16 [64, 128], replicated, may hold values from -3 to 3
- b_f1: float32 [128], replicated, may hold values from -3 to 3
- w_f2: bfloat16 [128, 128], replicated, may hold values from -0.1875 to 0.1875
- b_f2: float32 [128], replicated, may hold values from -2 to 2
- w_o1: bfloat16 [128, 128], replicated, may hold values from -0.25 to 0.25
- b_o1: float32 [128], replicated, may hold values from -3 to 3
- w_o2: bfloat16 [128, 128], replicated, may hold values from -0.5 to 0.5
- b_o2: float32 [128], replicated, may hold values from -3 to 3
- read_w: float32 [128], replicated, may hold values from -2 to 2
Outputs:
- features_out: bfloat16 [128, 4096], P(None, ('row', 'col'))
- forces: float32 [3, 4096], P(None, ('row', 'col'))
Inputs may be any that keep to these rules, and one draw needn't show every extreme that they name: Only slots 0 to pair_count[r, c] - 1 of tile_pairs and masks of block (r, c) are listed. tile_pairs[r, c, 0, s] is a receiver tile below 2, tile_pairs[r, c, 1, s] a sender tile below 16; the slots of one grid block hold distinct tile pairs.
All inputs are finite; a program needn't handle non-finite values. No bound on the sum of `masks` on one device may be relied on, other than what follows from the above.
Results may differ from a plain program's by a relative error of at most 0.0075.
Values may be sent and summed in bfloat16 or wider, within the bound.
No kernel may reach another device: no remote copies, remote signals or barrier semaphores. Data moves between devices by JAX's collectives and lax.ppermute only.
A program may use at most 64 MiB of HBM per device.

v0:
```python
import math

import jax
import jax.numpy as jnp
from jax import lax
from jax.experimental import pallas as pl
from jax.experimental.pallas import tpu as pltpu
from jax.sharding import PartitionSpec as P

SOFTENING = 0.25
GAMMA_RBF = 10.0
CENTER_MAX = 10.0
CUTOFF = 12.0
LN2 = math.log(2.0)
SCALE = math.sqrt(GAMMA_RBF / LN2)
TANGENT = -GAMMA_RBF / SCALE
POS_ROWS = 16
MIB = 1024 * 1024
F32 = jnp.float32
BF16 = jnp.bfloat16


def dot(a, b):
    return jnp.dot(a, b, preferred_element_type=F32)


def dot_t(a, b):
    return lax.dot_general(a, b, (((1,), (1,)), ((), ())), preferred_element_type=F32)


def split2(x):
    hi = x.astype(BF16)
    return hi, (x - hi.astype(F32)).astype(BF16)


def fold(x):
    half = x.shape[0] // 2
    return jnp.concatenate([x[:half], x[half:]], axis=1)


def unfold(x):
    half = x.shape[1] // 2
    return jnp.concatenate([x[:, :half], x[:, half:]], axis=0)


def block_diag(x):
    zero = jnp.zeros_like(x)
    return jnp.concatenate(
        [jnp.concatenate([x, zero], axis=1), jnp.concatenate([zero, x], axis=1)], axis=0
    )


def reverse_bits(value, count):
    bits = count.bit_length() - 1
    out = jnp.int32(0)
    for k in range(bits):
        out = out | (((value >> k) & 1) << (bits - 1 - k))
    return out


def out_type(shape, dtype):
    return pltpu.VMEM(shape, dtype)


def spread(row, count):
    rows = jnp.broadcast_to(row, (16, row.shape[1])).astype(BF16)
    return jnp.concatenate([rows] * (count // 16), axis=0)


def sin_cos(angle):
    turn = angle - 0.5 * math.pi
    square = turn * turn
    odd, even = 0.0, 0.0
    for k in range(6, -1, -1):
        odd = odd * square + (-1.0) ** k / math.factorial(2 * k + 1)
        even = even * square + (-1.0) ** k / math.factorial(2 * k)
    return even, -(odd * turn)


def fetch(sources, targets, sems):
    copies = [
        pltpu.make_async_copy(src, dst, sems.at[k])
        for k, (src, dst) in enumerate(zip(sources, targets))
    ]
    for copy in copies:
        copy.start()
    for copy in copies:
        copy.wait()


def pack_kernel(features_hbm, positions_hbm, out, col_pos, features, positions, sems):
    fetch([features_hbm, positions_hbm], [features, positions], sems)
    n_feat = features.shape[0]
    col_pos[0] = jnp.concatenate([positions[...], jnp.zeros((5, positions.shape[1]), F32)], axis=0)
    out[0, :n_feat] = features[...]
    exact = positions[...]
    hi = exact.astype(BF16).astype(F32)
    mid = (exact - hi).astype(BF16).astype(F32)
    pad = jnp.zeros((POS_ROWS - 9, exact.shape[1]), F32)
    pieces = jnp.concatenate([hi, mid, exact - hi - mid, pad], axis=0)
    out[0, n_feat:] = pieces.astype(BF16)


def stack_kernel(held, got, *rest):
    out = rest[-1]
    out[: held.shape[0]] = held[...]
    out[held.shape[0] :] = got[...]


def weight_kernel(
    w_in_hbm, w_f1_hbm, b_f1_hbm, w_f2_hbm, read_w_hbm, w_o2_hbm, w_o1_hbm, b_f2_hbm, b_o1_hbm, b_o2_hbm, masks_hbm, pairs_hbm,
    lhs, lhs_t, w2, w2_16, w_in_t, direction, w_o2, w_o1, b_f2, b_o1, b_o2, masks, pairs,
    w_in, w_f1, b_f1, w_f2, read_w, sems,
):
    fetch(
        [
            w_in_hbm, w_f1_hbm, b_f1_hbm, w_f2_hbm, read_w_hbm, w_o2_hbm,
            w_o1_hbm, b_f2_hbm, b_o1_hbm, b_o2_hbm, masks_hbm, pairs_hbm,
        ],
        [w_in, w_f1, b_f1, w_f2, read_w, w_o2, w_o1, b_f2, b_o1, b_o2, masks, pairs],
        sems,
    )
    nbasis, hidden = w_f1.shape
    weights = w_f1[...].astype(F32)
    bias = b_f1[...] * 0.5
    b_hi = bias.astype(BF16).astype(F32)
    b_mid = (bias - b_hi).astype(BF16).astype(F32)
    b_lo = bias - b_hi - b_mid
    extra = jnp.concatenate([b_hi, b_mid, b_lo, jnp.zeros((13, hidden), F32)], axis=0)
    table = jnp.concatenate(
        [
            jnp.concatenate([0.5 * weights, weights], axis=1),
            jnp.concatenate([extra, jnp.zeros_like(extra)], axis=1),
            jnp.zeros((128 - nbasis - 16, 2 * hidden), F32),
        ],
        axis=0,
    )
    flipped = table.T.astype(BF16)
    lhs[...] = flipped[:hidden, : nbasis + 16]
    lhs_t[...] = flipped[hidden:, :nbasis]
    wide = w_f2[...].astype(F32)
    w2[...] = jnp.concatenate([wide, wide], axis=1)
    w2_16[...] = w2[...].astype(BF16)
    w_in_t[...] = w_in[...].astype(F32).T.astype(BF16)
    readout = jnp.broadcast_to(read_w[...], (8, read_w.shape[1]))
    r_hi = readout.astype(BF16)
    r_mid, r_lo = split2(readout - r_hi.astype(F32))
    direction[...] = dot_t(r_hi, w_o2[...]) + (dot_t(r_mid, w_o2[...]) + dot_t(r_lo, w_o2[...]))


def pair_kernel(
    count, pairs, near, far, col_pos, masks, lhs, lhs_t, w2, w_in_t, b_f2,
    msg, msg16, tangents, proj_out, geom_out,
    diag, dist, coef_h, coef_x, rows, left,
):
    n_row = lax.axis_size("row")
    me_row = lax.axis_index("row")
    me_col = lax.axis_index("col")
    tile = masks.shape[2]
    hidden = w2.shape[0]
    nbasis = lhs.shape[1] - 16
    msg[...] = jnp.zeros_like(msg)
    centers = lax.broadcasted_iota(jnp.int32, (nbasis, 2 * tile), 0).astype(F32) * (
        SCALE * CENTER_MAX / (nbasis - 1)
    )
    ones = jnp.ones((16, 2 * tile), BF16)

    @pl.loop(0, count[0, 0])
    def _(slot):
        row_tile, col_tile = pairs[0, 0, 0, slot], pairs[0, 0, 1, slot]
        place = reverse_bits(col_tile ^ me_row, n_row)
        half = n_row // 2
        index = place & (half - 1)
        block = jnp.where(place >= half, far[index], near[index])
        proj = dot(w_in_t[...], block[:tile]).astype(BF16)
        proj_out[slot] = proj
        proj_t = proj.astype(F32).T.astype(BF16)
        diag[...] = block_diag(proj_t)
        pieces = block[tile:].astype(F32)
        sender = pieces[0:3] + pieces[3:6] + pieces[6:9]
        receiver = col_pos[row_tile ^ me_col]
        square = jnp.zeros((tile, tile), F32)
        separation = []
        for k in range(3):
            up = jnp.broadcast_to(receiver[k : k + 1], (tile, tile)).T
            separation.append(up - sender[k : k + 1])
            square = square + separation[k] * separation[k]
        distance = jnp.sqrt(square + SOFTENING)
        angle = (math.pi / CUTOFF) * distance
        mask = masks[slot].astype(F32)
        sine, cosine = sin_cos(angle)
        cut = 0.5 * (cosine + 1.0) * mask
        dist[...] = fold(distance * SCALE)
        coef_h[...] = fold(-LN2 * cut)
        coef_x[...] = fold(sine / (cosine + 1.0) * (LN2 * math.pi / CUTOFF / TANGENT))
        inverse = 1.0 / distance
        for k in range(3):
            geom_out[slot, k] = fold(separation[k] * inverse)
        geom_out[slot, 3] = fold((-0.5 * math.pi / CUTOFF) * sine * mask)
        geom_out[slot, 4] = fold(cut * TANGENT)
        c_hi, c_lo = split2(cut)
        bias_part = (dot(c_hi, proj_t) + dot(c_lo, proj_t)) * b_f2[...]

        d, h, x = dist[...], coef_h[...], coef_x[...]
        for u in range(tile // 2):
            offset = d[u : u + 1] - centers
            gauss = jnp.exp2(-(offset * offset))
            gauss = gauss.astype(BF16)
            basis = jnp.concatenate([gauss, ones], axis=0)
            bend = jnp.tanh(dot(lhs[...], basis))
            value = lax.log2(1.0 - bend).astype(BF16)
            along = dot(lhs_t[...], offset.astype(BF16) * gauss).astype(BF16)
            slope = (1.0 + bend).astype(BF16) * along
            left[pl.ds(u * hidden, hidden), :] = spread(h[u : u + 1], hidden) * value
            tangents[slot, u] = spread(x[u : u + 1], hidden) * value + slope
        mixed = dot(left[...], diag[...])
        sums = [
            jnp.sum(mixed[u * hidden : (u + 1) * hidden] * w2[...], axis=0, keepdims=True)
            for u in range(tile // 2)
        ]
        rows[...] = jnp.concatenate(sums, axis=0)

        here = pl.ds(pl.multiple_of(row_tile * tile, tile), tile)
        msg[here, :] = msg[here, :] + (bias_part + unfold(rows[...]))

    msg16[...] = msg[...].astype(BF16)


def force_kernel(
    count, pairs, msg_a, msg_b, near, w_o1, b_o1, w_o2, b_o2, direction, w2_16, b_f2,
    proj, geom, tangents,
    features_hbm, keep, send, row_keep, row_send,
    features_out, grads, pre_act, diag, rows, left, force, row_force, sems,
):
    n_row = lax.axis_size("row")
    n_col = lax.axis_size("col")
    me_row = lax.axis_index("row")
    me_col = lax.axis_index("col")
    n_feat, tile = features_out.shape
    hidden = w2_16.shape[0]
    force[...] = jnp.zeros_like(force)
    row_force[...] = jnp.zeros_like(row_force)
    messages = (msg_a[...] + msg_b[...].astype(F32)).astype(BF16)
    pre = dot(messages, w_o1[...]) + b_o1[...]
    pre_act[...] = pre
    s_hi, s_lo = split2(direction[0:1] / (1.0 + jnp.exp(-pre)))
    grads[...] = dot_t(s_hi, w_o1[...]) + dot_t(s_lo, w_o1[...])
    own = pre_act[pl.ds(pl.multiple_of(me_col * tile, tile), tile), :]
    active = jnp.maximum(own, 0.0) + jnp.log(1.0 + jnp.exp(-jnp.abs(own))) - LN2
    update = dot(active.astype(BF16), w_o2[...]) + b_o2[...]
    features_out[...] = (near[0, :n_feat].astype(F32) + update.T).astype(BF16)
    store = pltpu.make_async_copy(features_out, features_hbm, sems.at[0])
    store.start()

    @pl.loop(0, count[0, 0])
    def _(slot):
        row_tile, col_tile = pairs[0, 0, 0, slot], pairs[0, 0, 1, slot]
        here = pl.ds(pl.multiple_of(row_tile * tile, tile), tile)
        grad_rows = grads[here, :]
        left_rows = fold(grad_rows)
        rows[...] = left_rows
        diag[...] = block_diag(proj[slot])

        g = rows[...]
        for u in range(tile // 2):
            left[pl.ds(u * hidden, hidden), :] = w2_16[...] * spread(g[u : u + 1], hidden)
        mixed = dot(left[...], diag[...])
        sums = [
            jnp.sum(
                mixed[u * hidden : (u + 1) * hidden] * tangents[slot, u].astype(F32),
                axis=0,
                keepdims=True,
            )
            for u in range(tile // 2)
        ]
        rows[...] = jnp.concatenate(sums, axis=0)

        g_hi, g_lo = split2(grad_rows * b_f2[...])
        bias_part = dot(g_hi, proj[slot]) + dot(g_lo, proj[slot])
        dist_grad = unfold(geom[slot, 4] * rows[...]) + unfold(geom[slot, 3]) * bias_part
        to_rows, to_cols = [], []
        for k in range(3):
            push = unfold(geom[slot, k]) * dist_grad
            to_cols.append(jnp.sum(push, axis=0, keepdims=True))
            to_rows.append(-jnp.sum(push.T, axis=0, keepdims=True))
        zero = jnp.zeros((5, tile), F32)
        place = reverse_bits(col_tile ^ me_row, n_row)
        force[place] = force[place] + jnp.concatenate(to_cols + [zero], axis=0)
        place = reverse_bits(row_tile ^ me_col, n_col)
        row_force[place] = row_force[place] + jnp.concatenate(to_rows + [zero], axis=0)

    keep[...] = force[: n_row // 2]
    send[...] = force[n_row // 2 :]
    row_keep[...] = row_force[: n_col // 2]
    row_send[...] = row_force[n_col // 2 :]
    store.wait()


def exchange(value, axis, size, step):
    return lax.ppermute(value, axis, [(i, i ^ step) for i in range(size)])


ANY = pl.BlockSpec(memory_space=pl.ANY)
SMEM = pl.BlockSpec(memory_space=pltpu.SMEM)
VMEM = pl.BlockSpec(memory_space=pltpu.VMEM)
HBM = pl.BlockSpec(memory_space=pltpu.HBM)


def run(kernel, name, specs, out_shape, scratch, limit, *operands):
    return pl.pallas_call(
        kernel,
        in_specs=specs,
        out_specs=[pl.BlockSpec(memory_space=x.memory_space) for x in out_shape],
        out_shape=out_shape,
        scratch_shapes=scratch,
        compiler_params=pltpu.CompilerParams(vmem_limit_bytes=limit * MIB),
        name=name,
    )(*operands)


def local(
    features, positions, tile_pairs, pair_count, masks,
    w_in, w_f1, b_f1, w_f2, b_f2, w_o1, b_o1, w_o2, b_o2, read_w,
):
    n_feat, owned = features.shape
    tile = masks.shape[-1]
    tp = masks.shape[2]
    n_row = lax.axis_size("row")
    n_col = lax.axis_size("col")
    span = n_col * owned
    half = tile // 2
    nbasis, hidden = w_f1.shape

    near, col_pos = run(
        pack_kernel, "pack_tile", [HBM, HBM],
        [out_type((1, n_feat + POS_ROWS, owned), BF16), out_type((1, 8, owned), F32)],
        [
            pltpu.VMEM(features.shape, BF16),
            pltpu.VMEM(positions.shape, F32),
            pltpu.SemaphoreType.DMA((2,)),
        ],
        60,
        features, positions,
    )
    lhs, lhs_t, w2, w2_16, w_in_t, direction, w_o2, w_o1, b_f2, b_o1, b_o2, masks, pairs = run(
        weight_kernel, "weight_tables", [HBM] * 12,
        [
            out_type((hidden, nbasis + 16), BF16),
            out_type((hidden, nbasis), BF16),
            out_type((hidden, 2 * n_feat), F32),
            out_type((hidden, 2 * n_feat), BF16),
            out_type((n_feat, n_feat), BF16),
            out_type((8, n_feat), F32),
            out_type(w_o2.shape, BF16),
            out_type(w_o1.shape, BF16),
        ]
        + [out_type((1, n_feat), F32)] * 3
        + [out_type((tp, tile, tile), jnp.int32), pltpu.SMEM(tile_pairs.shape, jnp.int32)],
        [
            pltpu.VMEM(w_in.shape, BF16),
            pltpu.VMEM(w_f1.shape, BF16),
            pltpu.VMEM((1, hidden), F32),
            pltpu.VMEM(w_f2.shape, BF16),
            pltpu.VMEM((1, n_feat), F32),
            pltpu.SemaphoreType.DMA((12,)),
        ],
        60,
        w_in, w_f1, b_f1[None], w_f2, read_w[None], w_o2, w_o1, b_f2[None], b_o1[None], b_o2[None],
        masks[0, 0], tile_pairs,
    )
    col_pos = col_pos
    step = 1
    while step < n_col:
        col_pos = jnp.concatenate([col_pos, exchange(col_pos, "col", n_col, step)], axis=0)
        step *= 2

    def stack(held, got, *after):
        return run(
            stack_kernel, "stack_tiles", [VMEM, VMEM] + [ANY] * len(after),
            [out_type((2 * held.shape[0],) + held.shape[1:], BF16)], [], 4,
            held, got, *after,
        )[0]

    ready = [[w2], [col_pos]]
    own = near
    step = n_row // 2
    while step > 1:
        near = stack(near, exchange(near, "row", n_row, step), *(ready.pop(0) if ready else []))
        step //= 2
    far = exchange(near, "row", n_row, 1)
    count = pair_count

    plane = pltpu.VMEM((half, 2 * tile), F32)
    partial, partial16, tangents, proj, geom = run(
        pair_kernel, "pair_messages", [SMEM, SMEM] + [VMEM] * 9,
        [
            out_type((span, n_feat), F32),
            out_type((span, n_feat), BF16),
            out_type((tp, half, n_feat, 2 * tile), BF16),
            out_type((tp, n_feat, tile), BF16),
            out_type((tp, 5, half, 2 * tile), F32),
        ],
        [
            pltpu.VMEM((2 * tile, 2 * n_feat), BF16),
            plane, plane, plane, plane,
            pltpu.VMEM((half * hidden, 2 * tile), BF16),
        ],
        16,
        count, pairs, near, far, col_pos, masks, lhs, lhs_t, w2, w_in_t, b_f2,
    )

    step = 1
    while step < n_col // 2:
        partial = partial + exchange(partial16, "col", n_col, step).astype(F32)
        partial16 = partial.astype(BF16)
        step *= 2
    other = exchange(partial16, "col", n_col, step)

    features_out, keep, send, row_keep, row_send = run(
        force_kernel, "pair_forces",
        [SMEM, SMEM] + [VMEM] * 13,
        [
            pltpu.HBM((n_feat, owned), BF16),
            out_type((n_row // 2, 8, owned), F32),
            out_type((n_row // 2, 8, owned), F32),
            out_type((n_col // 2, 8, owned), F32),
            out_type((n_col // 2, 8, owned), F32),
        ],
        [
            pltpu.VMEM((n_feat, owned), BF16),
            pltpu.VMEM((span, n_feat), F32),
            pltpu.VMEM((span, n_feat), F32),
            pltpu.VMEM((2 * tile, 2 * n_feat), BF16),
            plane,
            pltpu.VMEM((half * hidden, 2 * n_feat), BF16),
            pltpu.VMEM((n_row, 8, owned), F32),
            pltpu.VMEM((n_col, 8, owned), F32),
            pltpu.SemaphoreType.DMA((1,)),
        ],
        16,
        count, pairs, partial, other, own, w_o1, b_o1, w_o2, b_o2, direction, w2_16, b_f2,
        proj, geom, tangents,
    )

    def reduce_halves(keep, send, axis, size):
        step = 1
        while True:
            other = exchange(send, axis, size, step)
            half = keep.shape[0] // 2
            step *= 2
            if step == size:
                return (keep + other)[0]
            send = keep[half:] + other[half:]
            keep = keep[:half] + other[:half]

    forces = reduce_halves(keep, send, "row", n_row) + reduce_halves(
        row_keep, row_send, "col", n_col
    )
    return (features_out, forces[:3])


def solution(mesh):
    atoms = P(None, ("row", "col"))
    in_specs = (
        atoms,
        atoms,
        P("row", "col", None, None),
        P("row", "col"),
        P("row", "col", None, None, None),
    ) + (P(),) * 10
    return jax.shard_map(
        local, mesh=mesh, in_specs=in_specs, out_specs=(atoms, atoms), check_vma=False
    )
```

profile of v0, /device:TPU:0, one launch (start us, length us, event | category | flops | bytes accessed | tf_op | source)
XLA Modules:
  0.0 62.9 jit_solution(9890778857109126129)
XLA Ops:
  0.6 0.8 %pack_tile.1 = (bf16[1,144,128]{2,1,0:T(8,128)(2,1)S(1)}, f32[1,8,128]{2,1,0:T(8,128)S(1)}) custom-call(bf16[128,128]{1,0:T(8,128)(2,1)} %features_hbm.1, f32[3,128]{1,0:T(4,128)} %positions_hbm.1), custom_call_target="tpu_custom_call" | custom-call | tf_op jit(solution)/shard_map/pack_tile/pallas_call | solution.py:310
  1.4 3.0 %collective-permute-start.2 = (f32[1,8,128]{2,1,0:T(8,128)S(1)}, f32[1,8,128]{2,1,0:T(8,128)S(1)}, u32[]{:S(2)}, u32[]{:S(2)}) collective-permute-start(f32[1,8,128]{2,1,0:T(8,128)S(1)} %get-tuple-element.30), channel_id=1, source_target_pairs={{0,1},{1,0},{2,3},{3,2},{4,5},{5,4},{6,7},{7,6},{8,9},{9,8},{10,11... | collective-permute-start | bytes 12296 | tf_op jit(solution)/shard_map/ppermute | solution.py:300
  4.4 2.6 %collective-permute-start = (bf16[1,144,128]{2,1,0:T(8,128)(2,1)S(1)}, bf16[1,144,128]{2,1,0:T(8,128)(2,1)S(1)}, u32[]{:S(2)}, u32[]{:S(2)}) collective-permute-start(bf16[1,144,128]{2,1,0:T(8,128)(2,1)S(1)} %get-tuple-element.28.held.near), channel_id=1, source_target_pairs={{0,16},{2,18},{4,20},{6,22},{8,24},{10,26},{12,28},{14,30},{16,0},... | collective-permute-start | bytes 110600 | tf_op jit(solution)/shard_map/ppermute | solution.py:300
  7.0 1.4 %weight_tables.1 = (bf16[128,80]{1,0:T(8,128)(2,1)S(1)}, bf16[128,64]{1,0:T(8,128)(2,1)S(1)}, f32[128,256]{1,0:T(8,128)S(1)}, bf16[128,256]{1,0:T(8,128)(2,1)S(1...) custom-call(bf16[128,128]{1,0:T(8,128)(2,1)} %w_in_hbm.1, ...), custom_call_target="tpu_custom_call" | custom-call | tf_op jit(solution)/shard_map/weight_tables/pallas_call | solution.py:310
  8.4 0.9 %collective-permute-done.got = bf16[1,144,128]{2,1,0:T(8,128)(2,1)S(1)} collective-permute-done((bf16[1,144,128]{2,1,0:T(8,128)(2,1)S(1)}, bf16[1,144,128]{2,1,0:T(8,128)(2,1)S(1)}, u32[]{:S(2)}, u32[]{:S(2)}) %collective-permute-start) | collective-permute-done | bytes 36896 | tf_op jit(solution)/shard_map/ppermute | solution.py:300
  9.3 1.6 %collective-permute-start.1 = (bf16[2,144,128]{2,1,0:T(8,128)(2,1)S(1)}, bf16[2,144,128]{2,1,0:T(8,128)(2,1)S(1)}, u32[]{:S(2)}, u32[]{:S(2)}) collective-permute-start(bf16[2,144,128]{2,1,0:T(8,128)(2,1)S(1)} %stack_tiles.3.held), channel_id=1, source_target_pairs={{0,8},{2,10},{4,12},{6,14},{8,0},{10,2},{12,4},{14,6},{16,24},{18,... | collective-permute-start | bytes 221192 | tf_op jit(solution)/shard_map/ppermute | solution.py:300
  10.9 0.0 collective-permute-done.2
  10.9 2.8 %collective-permute-done.1.got = bf16[2,144,128]{2,1,0:T(8,128)(2,1)S(1)} collective-permute-done((bf16[2,144,128]{2,1,0:T(8,128)(2,1)S(1)}, bf16[2,144,128]{2,1,0:T(8,128)(2,1)S(1)}, u32[]{:S(2)}, u32[]{:S(2)}) %collective-permute-start.1) | collective-permute-done | bytes 73760 | tf_op jit(solution)/shard_map/ppermute | solution.py:300
  13.7 1.6 %collective-permute-start.3 = (bf16[4,144,128]{2,1,0:T(8,128)(2,1)S(1)}, bf16[4,144,128]{2,1,0:T(8,128)(2,1)S(1)}, u32[]{:S(2)}, u32[]{:S(2)}) collective-permute-start(bf16[4,144,128]{2,1,0:T(8,128)(2,1)S(1)} %stack_tiles.4.held), channel_id=1, source_target_pairs={{0,4},{2,6},{4,0},{6,2},{8,12},{10,14},{12,8},{14,10},{16,20},{18,... | collective-permute-start | bytes 442376 | tf_op jit(solution)/shard_map/ppermute | solution.py:300
  15.2 3.6 %collective-permute-done.3.got = bf16[4,144,128]{2,1,0:T(8,128)(2,1)S(1)} collective-permute-done((bf16[4,144,128]{2,1,0:T(8,128)(2,1)S(1)}, bf16[4,144,128]{2,1,0:T(8,128)(2,1)S(1)}, u32[]{:S(2)}, u32[]{:S(2)}) %collective-permute-start.3) | collective-permute-done | bytes 147488 | tf_op jit(solution)/shard_map/ppermute | solution.py:300
  18.9 0.1 collective-permute-start.4
  19.6 0.9 %collective-permute-done.4.far = bf16[8,144,128]{2,1,0:T(8,128)(2,1)S(1)} collective-permute-done((bf16[8,144,128]{2,1,0:T(8,128)(2,1)S(1)}, bf16[8,144,128]{2,1,0:T(8,128)(2,1)S(1)}, u32[]{:S(2)}, u32[]{:S(2)}) %collective-permute-start.4) | collective-permute-done | bytes 294944 | tf_op jit(solution)/shard_map/ppermute | solution.py:300
  20.5 4.7 %pair_messages.1 = (f32[256,128]{1,0:T(8,128)S(1)}, bf16[256,128]{1,0:T(8,128)(2,1)S(1)}, bf16[4,64,128,256]{3,2,1,0:T(8,128)(2,1)S(1)}, bf16[4,128,128]{2,1,0:T(8,128)(2,1)S(1)}, f32[4,5,64,256]{3,2,1,0:T(8,128)S(1)}) custom-call(s32[1,1]{1,0:T(1,128)S(6)} %copy.18.count, s32[1,1,2,4]{3,2,1,0:T(2,128)S(4)} %get-tuple-element.27.pairs, ...), custom_call_target="tpu_custom_call" | custom-call | tf_op jit(solution)/shard_map/pair_messages/pallas_call | solution.py:310
  25.2 5.2 %collective-permute-start.5 = (bf16[256,128]{1,0:T(8,128)(2,1)S(1)}, bf16[256,128]{1,0:T(8,128)(2,1)S(1)}, u32[]{:S(2)}, u32[]{:S(2)}) collective-permute-start(bf16[256,128]{1,0:T(8,128)(2,1)S(1)} %get-tuple-element.37), channel_id=1, source_target_pairs={{0,1},{1,0},{2,3},{3,2},{4,5},{5,4},{6,7},{7,6},{8,9},{9,8},{10,11... | collective-permute-start | bytes 196616 | tf_op jit(solution)/shard_map/ppermute | solution.py:300
  30.4 2.4 %collective-permute-done.5.msg_b = bf16[256,128]{1,0:T(8,128)(2,1)S(1)} collective-permute-done((bf16[256,128]{1,0:T(8,128)(2,1)S(1)}, bf16[256,128]{1,0:T(8,128)(2,1)S(1)}, u32[]{:S(2)}, u32[]{:S(2)}) %collective-permute-start.5) | collective-permute-done | bytes 65568 | tf_op jit(solution)/shard_map/ppermute | solution.py:300
  32.8 2.0 %pair_forces.1 = (bf16[128,128]{1,0:T(8,128)(2,1)}, f32[8,8,128]{2,1,0:T(8,128)S(1)}, f32[8,8,128]{2,1,0:T(8,128)S(1)}, f32[1,8,128]{2,1,0:T(8,128)S(1)}, f32[1,8,128]{2,1,0:T(8,128)S(1)}) custom-call(s32[1,1]{1,0:T(1,128)S(6)} %copy.18.count, s32[1,1,2,4]{3,2,1,0:T(2,128)S(4)} %get-tuple-element.27.pairs, f32[256,128]{1,0:T(8,128)S(1)} %get-tuple-element.36.msg_a, ...), custom_call_target="tpu_custom_call" | custom-call | tf_op jit(solution)/shard_map/pair_forces/pallas_call | solution.py:310
  34.9 0.1 collective-permute-start.6
  35.0 1.2 %collective-permute-done.6 = f32[8,8,128]{2,1,0:T(8,128)S(1)} collective-permute-done((f32[8,8,128]{2,1,0:T(8,128)S(1)}, f32[8,8,128]{2,1,0:T(8,128)S(1)}, u32[]{:S(2)}, u32[]{:S(2)}) %collective-permute-start.6) | collective-permute-done | bytes 32800 | tf_op jit(solution)/shard_map/ppermute | solution.py:300
  36.2 3.1 %collective-permute-start.7 = (f32[4,8,128]{2,1,0:T(8,128)S(1)}, f32[4,8,128]{2,1,0:T(8,128)S(1)}, u32[]{:S(2)}, u32[]{:S(2)}) collective-permute-start(f32[4,8,128]{2,1,0:T(8,128)S(1)} %get-tuple-element.53), channel_id=1, source_target_pairs={{0,4},{2,6},{4,0},{6,2},{8,12},{10,14},{12,8},{14,10},{16,20},{18,... | collective-permute-start | bytes 49160 | tf_op jit(solution)/shard_map/ppermute | solution.py:300
  39.2 1.7 %collective-permute-done.7 = f32[4,8,128]{2,1,0:T(8,128)S(1)} collective-permute-done((f32[4,8,128]{2,1,0:T(8,128)S(1)}, f32[4,8,128]{2,1,0:T(8,128)S(1)}, u32[]{:S(2)}, u32[]{:S(2)}) %collective-permute-start.7) | collective-permute-done | bytes 16416 | tf_op jit(solution)/shard_map/ppermute | solution.py:300
  40.9 14.4 %collective-permute-start.8 = (f32[2,8,128]{2,1,0:T(8,128)S(1)}, f32[2,8,128]{2,1,0:T(8,128)S(1)}, u32[]{:S(2)}, u32[]{:S(2)}) collective-permute-start(f32[2,8,128]{2,1,0:T(8,128)S(1)} %get-tuple-element.55), channel_id=1, source_target_pairs={{0,8},{2,10},{4,12},{6,14},{8,0},{10,2},{12,4},{14,6},{16,24},{18,... | collective-permute-start | bytes 24584 | tf_op jit(solution)/shard_map/ppermute | solution.py:300
  55.4 0.0 collective-permute-start.10
  55.4 1.6 %collective-permute-done.8 = f32[2,8,128]{2,1,0:T(8,128)S(1)} collective-permute-done((f32[2,8,128]{2,1,0:T(8,128)S(1)}, f32[2,8,128]{2,1,0:T(8,128)S(1)}, u32[]{:S(2)}, u32[]{:S(2)}) %collective-permute-start.8) | collective-permute-done | bytes 8224 | tf_op jit(solution)/shard_map/ppermute | solution.py:300
  57.0 3.7 %collective-permute-start.9 = (f32[1,8,128]{2,1,0:T(8,128)S(1)}, f32[1,8,128]{2,1,0:T(8,128)S(1)}, u32[]{:S(2)}, u32[]{:S(2)}) collective-permute-start(f32[1,8,128]{2,1,0:T(8,128)S(1)} %slice_add_fusion.4), channel_id=1, source_target_pairs={{0,16},{2,18},{4,20},{6,22},{8,24},{10,26},{12,28},{14,30},{16,0},... | collective-permute-start | bytes 12296 | tf_op jit(solution)/shard_map/ppermute | solution.py:300
  60.7 0.0 collective-permute-done.10
  60.7 1.6 %collective-permute-done.9 = f32[1,8,128]{2,1,0:T(8,128)S(1)} collective-permute-done((f32[1,8,128]{2,1,0:T(8,128)S(1)}, f32[1,8,128]{2,1,0:T(8,128)S(1)}, u32[]{:S(2)}, u32[]{:S(2)}) %collective-permute-start.9) | collective-permute-done | bytes 4128 | tf_op jit(solution)/shard_map/ppermute | solution.py:300
  62.3 0.6 slice_bitcast_fusion
  (9 shorter events, 0.1 us)
Async XLA Ops:
  1.4 9.4 %collective-permute-start.2 = (f32[1,8,128]{2,1,0:T(8,128)S(1)}, f32[1,8,128]{2,1,0:T(8,128)S(1)}, u32[]{:S(2)}, u32[]{:S(2)}) collective-permute-start(f32[1,8,128]{2,1,0:T(8,128)S(1)} %get-tuple-element.30), channel_id=1, source_target_pairs={{0,1},{1,0},{2,3},{3,2},{4,5},{5,4},{6,7},{7,6},{8,9},{9,8},{10,11... | collective-permute-start | bytes 12296 | tf_op jit(solution)/shard_map/ppermute | solution.py:300
  4.4 4.9 %collective-permute-start = (bf16[1,144,128]{2,1,0:T(8,128)(2,1)S(1)}, bf16[1,144,128]{2,1,0:T(8,128)(2,1)S(1)}, u32[]{:S(2)}, u32[]{:S(2)}) collective-permute-start(bf16[1,144,128]{2,1,0:T(8,128)(2,1)S(1)} %get-tuple-element.28.held.near), channel_id=1, source_target_pairs={{0,16},{2,18},{4,20},{6,22},{8,24},{10,26},{12,28},{14,30},{16,0},... | collective-permute-start | bytes 110600 | tf_op jit(solution)/shard_map/ppermute | solution.py:300
  9.3 4.4 %collective-permute-start.1 = (bf16[2,144,128]{2,1,0:T(8,128)(2,1)S(1)}, bf16[2,144,128]{2,1,0:T(8,128)(2,1)S(1)}, u32[]{:S(2)}, u32[]{:S(2)}) collective-permute-start(bf16[2,144,128]{2,1,0:T(8,128)(2,1)S(1)} %stack_tiles.3.held), channel_id=1, source_target_pairs={{0,8},{2,10},{4,12},{6,14},{8,0},{10,2},{12,4},{14,6},{16,24},{18,... | collective-permute-start | bytes 221192 | tf_op jit(solution)/shard_map/ppermute | solution.py:300
  13.7 5.2 %collective-permute-start.3 = (bf16[4,144,128]{2,1,0:T(8,128)(2,1)S(1)}, bf16[4,144,128]{2,1,0:T(8,128)(2,1)S(1)}, u32[]{:S(2)}, u32[]{:S(2)}) collective-permute-start(bf16[4,144,128]{2,1,0:T(8,128)(2,1)S(1)} %stack_tiles.4.held), channel_id=1, source_target_pairs={{0,4},{2,6},{4,0},{6,2},{8,12},{10,14},{12,8},{14,10},{16,20},{18,... | collective-permute-start | bytes 442376 | tf_op jit(solution)/shard_map/ppermute | solution.py:300
  18.9 1.6 %collective-permute-start.4 = (bf16[8,144,128]{2,1,0:T(8,128)(2,1)S(1)}, bf16[8,144,128]{2,1,0:T(8,128)(2,1)S(1)}, u32[]{:S(2)}, u32[]{:S(2)}) collective-permute-start(bf16[8,144,128]{2,1,0:T(8,128)(2,1)S(1)} %stack_tiles.5.near), channel_id=1, source_target_pairs={{0,2},{2,0},{4,6},{6,4},{8,10},{10,8},{12,14},{14,12},{16,18},{18,... | collective-permute-start | bytes 884744 | tf_op jit(solution)/shard_map/ppermute | solution.py:300
  25.2 7.6 %collective-permute-start.5 = (bf16[256,128]{1,0:T(8,128)(2,1)S(1)}, bf16[256,128]{1,0:T(8,128)(2,1)S(1)}, u32[]{:S(2)}, u32[]{:S(2)}) collective-permute-start(bf16[256,128]{1,0:T(8,128)(2,1)S(1)} %get-tuple-element.37), channel_id=1, source_target_pairs={{0,1},{1,0},{2,3},{3,2},{4,5},{5,4},{6,7},{7,6},{8,9},{9,8},{10,11... | collective-permute-start | bytes 196616 | tf_op jit(solution)/shard_map/ppermute | solution.py:300
  34.9 1.3 %collective-permute-start.6 = (f32[8,8,128]{2,1,0:T(8,128)S(1)}, f32[8,8,128]{2,1,0:T(8,128)S(1)}, u32[]{:S(2)}, u32[]{:S(2)}) collective-permute-start(f32[8,8,128]{2,1,0:T(8,128)S(1)} %get-tuple-element.49), channel_id=1, source_target_pairs={{0,2},{2,0},{4,6},{6,4},{8,10},{10,8},{12,14},{14,12},{16,18},{18,... | collective-permute-start | bytes 98312 | tf_op jit(solution)/shard_map/ppermute | solution.py:300
  36.2 4.8 %collective-permute-start.7 = (f32[4,8,128]{2,1,0:T(8,128)S(1)}, f32[4,8,128]{2,1,0:T(8,128)S(1)}, u32[]{:S(2)}, u32[]{:S(2)}) collective-permute-start(f32[4,8,128]{2,1,0:T(8,128)S(1)} %get-tuple-element.53), channel_id=1, source_target_pairs={{0,4},{2,6},{4,0},{6,2},{8,12},{10,14},{12,8},{14,10},{16,20},{18,... | collective-permute-start | bytes 49160 | tf_op jit(solution)/shard_map/ppermute | solution.py:300
  40.9 16.0 %collective-permute-start.8 = (f32[2,8,128]{2,1,0:T(8,128)S(1)}, f32[2,8,128]{2,1,0:T(8,128)S(1)}, u32[]{:S(2)}, u32[]{:S(2)}) collective-permute-start(f32[2,8,128]{2,1,0:T(8,128)S(1)} %get-tuple-element.55), channel_id=1, source_target_pairs={{0,8},{2,10},{4,12},{6,14},{8,0},{10,2},{12,4},{14,6},{16,24},{18,... | collective-permute-start | bytes 24584 | tf_op jit(solution)/shard_map/ppermute | solution.py:300
  55.4 5.4 %collective-permute-start.10 = (f32[1,8,128]{2,1,0:T(8,128)S(1)}, f32[1,8,128]{2,1,0:T(8,128)S(1)}, u32[]{:S(2)}, u32[]{:S(2)}) collective-permute-start(f32[1,8,128]{2,1,0:T(8,128)S(1)} %get-tuple-element.51), channel_id=1, source_target_pairs={{0,1},{1,0},{2,3},{3,2},{4,5},{5,4},{6,7},{7,6},{8,9},{9,8},{10,11... | collective-permute-start | bytes 12296 | tf_op jit(solution)/shard_map/ppermute | solution.py:300
  57.0 5.3 %collective-permute-start.9 = (f32[1,8,128]{2,1,0:T(8,128)S(1)}, f32[1,8,128]{2,1,0:T(8,128)S(1)}, u32[]{:S(2)}, u32[]{:S(2)}) collective-permute-start(f32[1,8,128]{2,1,0:T(8,128)S(1)} %slice_add_fusion.4), channel_id=1, source_target_pairs={{0,16},{2,18},{4,20},{6,22},{8,24},{10,26},{12,28},{14,30},{16,0},... | collective-permute-start | bytes 12296 | tf_op jit(solution)/shard_map/ppermute | solution.py:300
where the time goes:
time: 63.5 us; the launch traced here: 62.9 us
  starting transfers between devices  35.3 us (56%)
  waiting for transfers between devices  16.7 us (26%)
  Pallas kernels  8.93 us (14%)
  between operations  1.34 us (2%)
    ppermute x11, starting transfers between devices, exchange(): return lax.ppermute(value, axis, [(i, i ^ step) for i in range(size)])  35.3 us
    ppermute x11, waiting for transfers between devices, exchange(): return lax.ppermute(value, axis, [(i, i ^ step) for i in range(size)])  16.7 us
    pallas_call x7, Pallas kernels, run(): pl.pallas_call(kernel, in_specs=specs, out_specs=[pl.BlockSpec(memory_spa...  8.93 us
  transfers between devices with their start and end apart: 11, of which 9 were waited for; matrix products, arithmetic and copies ran while one was open for 0% of the time, Pallas kernels for 2%

commit v1 on v0

--- a/solution.py
+++ b/solution.py
@@ -60,6 +60,18 @@
 
 def out_type(shape, dtype):
     return pltpu.VMEM(shape, dtype)
+
+
+def stage_orders(n_row):
+    steps = [n_row >> k for k in range(1, n_row.bit_length() - 1)]
+    return steps, steps[-1:] + steps[:-1]
+
+
+def stage_bits(value, steps):
+    out = jnp.int32(0)
+    for k, step in enumerate(steps):
+        out = out | (((value >> (step.bit_length() - 1)) & 1) << k)
+    return out
 
 
 def spread(row, count):
@@ -168,10 +180,11 @@
     @pl.loop(0, count[0, 0])
     def _(slot):
         row_tile, col_tile = pairs[0, 0, 0, slot], pairs[0, 0, 1, slot]
-        place = reverse_bits(col_tile ^ me_row, n_row)
-        half = n_row // 2
-        index = place & (half - 1)
-        block = jnp.where(place >= half, far[index], near[index])
+        apart = col_tile ^ me_row
+        even, odd = (stage_bits(apart, order) for order in stage_orders(n_row))
+        is_odd = (me_row & 1) == 1
+        mine, other = jnp.where(is_odd, odd, even), jnp.where(is_odd, even, odd)
+        block = jnp.where((apart & 1) == 1, far[other], near[mine])
         proj = dot(w_in_t[...], block[:tile]).astype(BF16)
         proj_out[slot] = proj
         proj_t = proj.astype(F32).T.astype(BF16)
@@ -283,7 +296,7 @@
             push = unfold(geom[slot, k]) * dist_grad
             to_cols.append(jnp.sum(push, axis=0, keepdims=True))
             to_rows.append(-jnp.sum(push.T, axis=0, keepdims=True))
-        zero = jnp.zeros((5, tile), F32)
+        zero = jnp.zeros((1, tile), F32)
         place = reverse_bits(col_tile ^ me_row, n_row)
         force[place] = force[place] + jnp.concatenate(to_cols + [zero], axis=0)
         place = reverse_bits(row_tile ^ me_col, n_col)
@@ -383,10 +396,10 @@
 
     ready = [[w2], [col_pos]]
     own = near
-    step = n_row // 2
-    while step > 1:
-        near = stack(near, exchange(near, "row", n_row, step), *(ready.pop(0) if ready else []))
-        step //= 2
+    for steps in zip(*stage_orders(n_row)):
+        pairs_of_rows = [(i, i ^ steps[i % 2]) for i in range(n_row)]
+        got = lax.ppermute(near, "row", pairs_of_rows)
+        near = stack(near, got, *(ready.pop(0) if ready else []))
     far = exchange(near, "row", n_row, 1)
     count = pair_count
 
@@ -421,10 +434,10 @@
         [SMEM, SMEM] + [VMEM] * 13,
         [
             pltpu.HBM((n_feat, owned), BF16),
-            out_type((n_row // 2, 8, owned), F32),
-            out_type((n_row // 2, 8, owned), F32),
-            out_type((n_col // 2, 8, owned), F32),
-            out_type((n_col // 2, 8, owned), F32),
+            out_type((n_row // 2, 4, owned), F32),
+            out_type((n_row // 2, 4, owned), F32),
+            out_type((n_col // 2, 4, owned), F32),
+            out_type((n_col // 2, 4, owned), F32),
         ],
         [
             pltpu.VMEM((n_feat, owned), BF16),
@@ -433,8 +446,8 @@
             pltpu.VMEM((2 * tile, 2 * n_feat), BF16),
             plane,
             pltpu.VMEM((half * hidden, 2 * n_feat), BF16),
-            pltpu.VMEM((n_row, 8, owned), F32),
-            pltpu.VMEM((n_col, 8, owned), F32),
+            pltpu.VMEM((n_row, 4, owned), F32),
+            pltpu.VMEM((n_col, 4, owned), F32),
             pltpu.SemaphoreType.DMA((1,)),
         ],
         16,

time: 63.5 us -> 63.2 us (level)
  starting transfers between devices: 35.3 us -> 24.8 us
  Pallas kernels: 8.93 us -> 15.1 us
  waiting for transfers between devices: 16.7 us -> 20.8 us
    ppermute x11 -> x8, starting transfers between devices: 35.3 us -> 19.1 us  [exchange(): return lax.ppermute(value, axis, [(i, i ^ step) for i in range(size)])]
    ppermute x0 -> x3, waiting for transfers between devices: none -> 7.34 us  [local(): got = lax.ppermute(near, 'row', pairs_of_rows)]
    pallas_call x7, Pallas kernels: 8.93 us -> 15.1 us  [run(): pl.pallas_call(kernel, in_specs=specs, out_specs=[pl.BlockSpec(memory_spa...]
    ppermute x0 -> x3, starting transfers between devices: none -> 5.75 us  [local(): got = lax.ppermute(near, 'row', pairs_of_rows)]
    ppermute x11 -> x8, waiting for transfers between devices: 16.7 us -> 13.5 us  [exchange(): return lax.ppermute(value, axis, [(i, i ^ step) for i in range(size)])]
where the time goes in v1:
time: 63.2 us; the launch traced here: 62.7 us
  starting transfers between devices  24.8 us (39%)
  waiting for transfers between devices  20.8 us (33%)
  Pallas kernels  15.1 us (24%)
  between operations  1.34 us (2%)
    ppermute x8, starting transfers between devices, exchange(): return lax.ppermute(value, axis, [(i, i ^ step) for i in range(size)])  19.1 us
    pallas_call x7, Pallas kernels, run(): pl.pallas_call(kernel, in_specs=specs, out_specs=[pl.BlockSpec(memory_spa...  15.1 us
    ppermute x8, waiting for transfers between devices, exchange(): return lax.ppermute(value, axis, [(i, i ^ step) for i in range(size)])  13.5 us
    ppermute x3, waiting for transfers between devices, local(): got = lax.ppermute(near, 'row', pairs_of_rows)  7.34 us
    ppermute x3, starting transfers between devices, local(): got = lax.ppermute(near, 'row', pairs_of_rows)  5.75 us
  transfers between devices with their start and end apart: 11, of which 9 were waited for; matrix products, arithmetic and copies ran while one was open for 0% of the time, Pallas kernels for 2%

profile of v1, /device:TPU:0, one launch (start us, length us, event | category | flops | bytes accessed | tf_op | source)
XLA Modules:
  0.0 62.7 jit_solution(13842394143493056907)
XLA Ops:
  0.6 0.8 %pack_tile.1 = (bf16[1,144,128]{2,1,0:T(8,128)(2,1)S(1)}, f32[1,8,128]{2,1,0:T(8,128)S(1)}) custom-call(bf16[128,128]{1,0:T(8,128)(2,1)} %features_hbm.1, f32[3,128]{1,0:T(4,128)} %positions_hbm.1), custom_call_target="tpu_custom_call" | custom-call | tf_op jit(solution)/shard_map/pack_tile/pallas_call | solution.py:323
  1.4 3.0 %collective-permute-start.2 = (f32[1,8,128]{2,1,0:T(8,128)S(1)}, f32[1,8,128]{2,1,0:T(8,128)S(1)}, u32[]{:S(2)}, u32[]{:S(2)}) collective-permute-start(f32[1,8,128]{2,1,0:T(8,128)S(1)} %get-tuple-element.30), channel_id=1, source_target_pairs={{0,1},{1,0},{2,3},{3,2},{4,5},{5,4},{6,7},{7,6},{8,9},{9,8},{10,11... | collective-permute-start | bytes 12296 | tf_op jit(solution)/shard_map/ppermute | solution.py:313
  4.4 2.6 %collective-permute-start = (bf16[1,144,128]{2,1,0:T(8,128)(2,1)S(1)}, bf16[1,144,128]{2,1,0:T(8,128)(2,1)S(1)}, u32[]{:S(2)}, u32[]{:S(2)}) collective-permute-start(bf16[1,144,128]{2,1,0:T(8,128)(2,1)S(1)} %get-tuple-element.28.held.near), channel_id=1, source_target_pairs={{0,16},{2,6},{4,20},{6,2},{8,24},{10,14},{12,28},{14,10},{16,0},{1... | collective-permute-start | bytes 110600 | tf_op jit(solution)/shard_map/ppermute | solution.py:401
  7.0 1.4 %weight_tables.1 = (bf16[128,80]{1,0:T(8,128)(2,1)S(1)}, bf16[128,64]{1,0:T(8,128)(2,1)S(1)}, f32[128,256]{1,0:T(8,128)S(1)}, bf16[128,256]{1,0:T(8,128)(2,1)S(1...) custom-call(bf16[128,128]{1,0:T(8,128)(2,1)} %w_in_hbm.1, ...), custom_call_target="tpu_custom_call" | custom-call | tf_op jit(solution)/shard_map/weight_tables/pallas_call | solution.py:323
  8.4 0.9 %collective-permute-done.got = bf16[1,144,128]{2,1,0:T(8,128)(2,1)S(1)} collective-permute-done((bf16[1,144,128]{2,1,0:T(8,128)(2,1)S(1)}, bf16[1,144,128]{2,1,0:T(8,128)(2,1)S(1)}, u32[]{:S(2)}, u32[]{:S(2)}) %collective-permute-start) | collective-permute-done | bytes 36896 | tf_op jit(solution)/shard_map/ppermute | solution.py:401
  9.3 1.6 %collective-permute-start.1 = (bf16[2,144,128]{2,1,0:T(8,128)(2,1)S(1)}, bf16[2,144,128]{2,1,0:T(8,128)(2,1)S(1)}, u32[]{:S(2)}, u32[]{:S(2)}) collective-permute-start(bf16[2,144,128]{2,1,0:T(8,128)(2,1)S(1)} %stack_tiles.3.held), channel_id=1, source_target_pairs={{0,8},{2,18},{4,12},{6,22},{8,0},{10,26},{12,4},{14,30},{16,24},{1... | collective-permute-start | bytes 221192 | tf_op jit(solution)/shard_map/ppermute | solution.py:401
  10.9 0.0 collective-permute-done.2
  10.9 2.9 %collective-permute-done.1.got = bf16[2,144,128]{2,1,0:T(8,128)(2,1)S(1)} collective-permute-done((bf16[2,144,128]{2,1,0:T(8,128)(2,1)S(1)}, bf16[2,144,128]{2,1,0:T(8,128)(2,1)S(1)}, u32[]{:S(2)}, u32[]{:S(2)}) %collective-permute-start.1) | collective-permute-done | bytes 73760 | tf_op jit(solution)/shard_map/ppermute | solution.py:401
  13.7 1.6 %collective-permute-start.3 = (bf16[4,144,128]{2,1,0:T(8,128)(2,1)S(1)}, bf16[4,144,128]{2,1,0:T(8,128)(2,1)S(1)}, u32[]{:S(2)}, u32[]{:S(2)}) collective-permute-start(bf16[4,144,128]{2,1,0:T(8,128)(2,1)S(1)} %stack_tiles.4.held), channel_id=1, source_target_pairs={{0,4},{2,10},{4,0},{6,14},{8,12},{10,2},{12,8},{14,6},{16,20},{18,... | collective-permute-start | bytes 442376 | tf_op jit(solution)/shard_map/ppermute | solution.py:401
  15.3 3.6 %collective-permute-done.3.got = bf16[4,144,128]{2,1,0:T(8,128)(2,1)S(1)} collective-permute-done((bf16[4,144,128]{2,1,0:T(8,128)(2,1)S(1)}, bf16[4,144,128]{2,1,0:T(8,128)(2,1)S(1)}, u32[]{:S(2)}, u32[]{:S(2)}) %collective-permute-start.3) | collective-permute-done | bytes 147488 | tf_op jit(solution)/shard_map/ppermute | solution.py:401
  19.0 0.1 collective-permute-start.4
  19.7 0.9 %collective-permute-done.4.far = bf16[8,144,128]{2,1,0:T(8,128)(2,1)S(1)} collective-permute-done((bf16[8,144,128]{2,1,0:T(8,128)(2,1)S(1)}, bf16[8,144,128]{2,1,0:T(8,128)(2,1)S(1)}, u32[]{:S(2)}, u32[]{:S(2)}) %collective-permute-start.4) | collective-permute-done | bytes 294944 | tf_op jit(solution)/shard_map/ppermute | solution.py:313
  20.6 9.3 %pair_messages.1 = (f32[256,128]{1,0:T(8,128)S(1)}, bf16[256,128]{1,0:T(8,128)(2,1)S(1)}, bf16[4,64,128,256]{3,2,1,0:T(8,128)(2,1)S(1)}, bf16[4,128,128]{2,1,0:T(8,128)(2,1)S(1)}, f32[4,5,64,256]{3,2,1,0:T(8,128)S(1)}) custom-call(s32[1,1]{1,0:T(1,128)S(6)} %copy.18.count, s32[1,1,2,4]{3,2,1,0:T(2,128)S(4)} %get-tuple-element.27.pairs, ...), custom_call_target="tpu_custom_call" | custom-call | tf_op jit(solution)/shard_map/pair_messages/pallas_call | solution.py:323
  29.9 0.2 collective-permute-start.5
  30.1 4.1 %collective-permute-done.5.msg_b = bf16[256,128]{1,0:T(8,128)(2,1)S(1)} collective-permute-done((bf16[256,128]{1,0:T(8,128)(2,1)S(1)}, bf16[256,128]{1,0:T(8,128)(2,1)S(1)}, u32[]{:S(2)}, u32[]{:S(2)}) %collective-permute-start.5) | collective-permute-done | bytes 65568 | tf_op jit(solution)/shard_map/ppermute | solution.py:313
  34.3 3.6 %pair_forces.1 = (bf16[128,128]{1,0:T(8,128)(2,1)}, f32[8,4,128]{2,1,0:T(4,128)S(1)}, f32[8,4,128]{2,1,0:T(4,128)S(1)}, f32[1,4,128]{2,1,0:T(4,128)S(1)}, f32[1,4,128]{2,1,0:T(4,128)S(1)}) custom-call(s32[1,1]{1,0:T(1,128)S(6)} %copy.18.count, s32[1,1,2,4]{3,2,1,0:T(2,128)S(4)} %get-tuple-element.27.pairs, f32[256,128]{1,0:T(8,128)S(1)} %get-tuple-element.36.msg_a, ...), custom_call_target="tpu_custom_call" | custom-call | tf_op jit(solution)/shard_map/pair_forces/pallas_call | solution.py:323
  37.9 0.1 collective-permute-start.6
  37.9 1.2 %collective-permute-done.6 = f32[8,4,128]{2,1,0:T(4,128)S(1)} collective-permute-done((f32[8,4,128]{2,1,0:T(4,128)S(1)}, f32[8,4,128]{2,1,0:T(4,128)S(1)}, u32[]{:S(2)}, u32[]{:S(2)}) %collective-permute-start.6) | collective-permute-done | bytes 16416 | tf_op jit(solution)/shard_map/ppermute | solution.py:313
  39.1 0.1 collective-permute-start.7
  39.2 3.5 %collective-permute-done.7 = f32[4,4,128]{2,1,0:T(4,128)S(1)} collective-permute-done((f32[4,4,128]{2,1,0:T(4,128)S(1)}, f32[4,4,128]{2,1,0:T(4,128)S(1)}, u32[]{:S(2)}, u32[]{:S(2)}) %collective-permute-start.7) | collective-permute-done | bytes 8224 | tf_op jit(solution)/shard_map/ppermute | solution.py:313
  42.8 1.4 %collective-permute-start.8 = (f32[2,4,128]{2,1,0:T(4,128)S(1)}, f32[2,4,128]{2,1,0:T(4,128)S(1)}, u32[]{:S(2)}, u32[]{:S(2)}) collective-permute-start(f32[2,4,128]{2,1,0:T(4,128)S(1)} %get-tuple-element.55), channel_id=1, source_target_pairs={{0,8},{2,10},{4,12},{6,14},{8,0},{10,2},{12,4},{14,6},{16,24},{18,... | collective-permute-start | bytes 12296 | tf_op jit(solution)/shard_map/ppermute | solution.py:313
  44.2 0.0 collective-permute-start.10
  44.2 2.2 %collective-permute-done.8 = f32[2,4,128]{2,1,0:T(4,128)S(1)} collective-permute-done((f32[2,4,128]{2,1,0:T(4,128)S(1)}, f32[2,4,128]{2,1,0:T(4,128)S(1)}, u32[]{:S(2)}, u32[]{:S(2)}) %collective-permute-start.8) | collective-permute-done | bytes 4128 | tf_op jit(solution)/shard_map/ppermute | solution.py:313
  46.4 14.2 %collective-permute-start.9 = (f32[1,4,128]{2,1,0:T(4,128)S(1)}, f32[1,4,128]{2,1,0:T(4,128)S(1)}, u32[]{:S(2)}, u32[]{:S(2)}) collective-permute-start(f32[1,4,128]{2,1,0:T(4,128)S(1)} %slice_add_fusion.4), channel_id=1, source_target_pairs={{0,16},{2,18},{4,20},{6,22},{8,24},{10,26},{12,28},{14,30},{16,0},... | collective-permute-start | bytes 6152 | tf_op jit(solution)/shard_map/ppermute | solution.py:313
  60.6 0.0 collective-permute-done.10
  60.6 1.6 %collective-permute-done.9 = f32[1,4,128]{2,1,0:T(4,128)S(1)} collective-permute-done((f32[1,4,128]{2,1,0:T(4,128)S(1)}, f32[1,4,128]{2,1,0:T(4,128)S(1)}, u32[]{:S(2)}, u32[]{:S(2)}) %collective-permute-start.9) | collective-permute-done | bytes 2080 | tf_op jit(solution)/shard_map/ppermute | solution.py:313
  62.1 0.6 slice_bitcast_fusion
  (9 shorter events, 0.1 us)
Async XLA Ops:
  1.4 9.4 %collective-permute-start.2 = (f32[1,8,128]{2,1,0:T(8,128)S(1)}, f32[1,8,128]{2,1,0:T(8,128)S(1)}, u32[]{:S(2)}, u32[]{:S(2)}) collective-permute-start(f32[1,8,128]{2,1,0:T(8,128)S(1)} %get-tuple-element.30), channel_id=1, source_target_pairs={{0,1},{1,0},{2,3},{3,2},{4,5},{5,4},{6,7},{7,6},{8,9},{9,8},{10,11... | collective-permute-start | bytes 12296 | tf_op jit(solution)/shard_map/ppermute | solution.py:313
  4.4 4.9 %collective-permute-start = (bf16[1,144,128]{2,1,0:T(8,128)(2,1)S(1)}, bf16[1,144,128]{2,1,0:T(8,128)(2,1)S(1)}, u32[]{:S(2)}, u32[]{:S(2)}) collective-permute-start(bf16[1,144,128]{2,1,0:T(8,128)(2,1)S(1)} %get-tuple-element.28.held.near), channel_id=1, source_target_pairs={{0,16},{2,6},{4,20},{6,2},{8,24},{10,14},{12,28},{14,10},{16,0},{1... | collective-permute-start | bytes 110600 | tf_op jit(solution)/shard_map/ppermute | solution.py:401
  9.3 4.4 %collective-permute-start.1 = (bf16[2,144,128]{2,1,0:T(8,128)(2,1)S(1)}, bf16[2,144,128]{2,1,0:T(8,128)(2,1)S(1)}, u32[]{:S(2)}, u32[]{:S(2)}) collective-permute-start(bf16[2,144,128]{2,1,0:T(8,128)(2,1)S(1)} %stack_tiles.3.held), channel_id=1, source_target_pairs={{0,8},{2,18},{4,12},{6,22},{8,0},{10,26},{12,4},{14,30},{16,24},{1... | collective-permute-start | bytes 221192 | tf_op jit(solution)/shard_map/ppermute | solution.py:401
  13.7 5.2 %collective-permute-start.3 = (bf16[4,144,128]{2,1,0:T(8,128)(2,1)S(1)}, bf16[4,144,128]{2,1,0:T(8,128)(2,1)S(1)}, u32[]{:S(2)}, u32[]{:S(2)}) collective-permute-start(bf16[4,144,128]{2,1,0:T(8,128)(2,1)S(1)} %stack_tiles.4.held), channel_id=1, source_target_pairs={{0,4},{2,10},{4,0},{6,14},{8,12},{10,2},{12,8},{14,6},{16,20},{18,... | collective-permute-start | bytes 442376 | tf_op jit(solution)/shard_map/ppermute | solution.py:401
  19.0 1.6 %collective-permute-start.4 = (bf16[8,144,128]{2,1,0:T(8,128)(2,1)S(1)}, bf16[8,144,128]{2,1,0:T(8,128)(2,1)S(1)}, u32[]{:S(2)}, u32[]{:S(2)}) collective-permute-start(bf16[8,144,128]{2,1,0:T(8,128)(2,1)S(1)} %stack_tiles.5.near), channel_id=1, source_target_pairs={{0,2},{2,0},{4,6},{6,4},{8,10},{10,8},{12,14},{14,12},{16,18},{18,... | collective-permute-start | bytes 884744 | tf_op jit(solution)/shard_map/ppermute | solution.py:313
  29.9 4.3 %collective-permute-start.5 = (bf16[256,128]{1,0:T(8,128)(2,1)S(1)}, bf16[256,128]{1,0:T(8,128)(2,1)S(1)}, u32[]{:S(2)}, u32[]{:S(2)}) collective-permute-start(bf16[256,128]{1,0:T(8,128)(2,1)S(1)} %get-tuple-element.37), channel_id=1, source_target_pairs={{0,1},{1,0},{2,3},{3,2},{4,5},{5,4},{6,7},{7,6},{8,9},{9,8},{10,11... | collective-permute-start | bytes 196616 | tf_op jit(solution)/shard_map/ppermute | solution.py:313
  37.9 1.2 %collective-permute-start.6 = (f32[8,4,128]{2,1,0:T(4,128)S(1)}, f32[8,4,128]{2,1,0:T(4,128)S(1)}, u32[]{:S(2)}, u32[]{:S(2)}) collective-permute-start(f32[8,4,128]{2,1,0:T(4,128)S(1)} %get-tuple-element.49), channel_id=1, source_target_pairs={{0,2},{2,0},{4,6},{6,4},{8,10},{10,8},{12,14},{14,12},{16,18},{18,... | collective-permute-start | bytes 49160 | tf_op jit(solution)/shard_map/ppermute | solution.py:313
  39.1 3.7 %collective-permute-start.7 = (f32[4,4,128]{2,1,0:T(4,128)S(1)}, f32[4,4,128]{2,1,0:T(4,128)S(1)}, u32[]{:S(2)}, u32[]{:S(2)}) collective-permute-start(f32[4,4,128]{2,1,0:T(4,128)S(1)} %get-tuple-element.53), channel_id=1, source_target_pairs={{0,4},{2,6},{4,0},{6,2},{8,12},{10,14},{12,8},{14,10},{16,20},{18,... | collective-permute-start | bytes 24584 | tf_op jit(solution)/shard_map/ppermute | solution.py:313
  42.8 3.6 %collective-permute-start.8 = (f32[2,4,128]{2,1,0:T(4,128)S(1)}, f32[2,4,128]{2,1,0:T(4,128)S(1)}, u32[]{:S(2)}, u32[]{:S(2)}) collective-permute-start(f32[2,4,128]{2,1,0:T(4,128)S(1)} %get-tuple-element.55), channel_id=1, source_target_pairs={{0,8},{2,10},{4,12},{6,14},{8,0},{10,2},{12,4},{14,6},{16,24},{18,... | collective-permute-start | bytes 12296 | tf_op jit(solution)/shard_map/ppermute | solution.py:313
  44.2 16.3 %collective-permute-start.10 = (f32[1,4,128]{2,1,0:T(4,128)S(1)}, f32[1,4,128]{2,1,0:T(4,128)S(1)}, u32[]{:S(2)}, u32[]{:S(2)}) collective-permute-start(f32[1,4,128]{2,1,0:T(4,128)S(1)} %get-tuple-element.51), channel_id=1, source_target_pairs={{0,1},{1,0},{2,3},{3,2},{4,5},{5,4},{6,7},{7,6},{8,9},{9,8},{10,11... | collective-permute-start | bytes 6152 | tf_op jit(solution)/shard_map/ppermute | solution.py:313
  46.4 15.7 %collective-permute-start.9 = (f32[1,4,128]{2,1,0:T(4,128)S(1)}, f32[1,4,128]{2,1,0:T(4,128)S(1)}, u32[]{:S(2)}, u32[]{:S(2)}) collective-permute-start(f32[1,4,128]{2,1,0:T(4,128)S(1)} %slice_add_fusion.4), channel_id=1, source_target_pairs={{0,16},{2,18},{4,20},{6,22},{8,24},{10,26},{12,28},{14,30},{16,0},... | collective-permute-start | bytes 6152 | tf_op jit(solution)/shard_map/ppermute | solution.py:313
